TPU v7x, 32 devices: a whole 2x2x4 slice. The times are simulated.
32 devices in a mesh: dp: 8 (over y, x, core), tensor: 4 (over z).
Axes of the slice: x: 2, y: 2, z: 4, core: 2. Of those that a mesh axis runs over, the one named last changes fastest.
Arguments:
- query: bfloat16 [128, 4096], P('dp', 'tensor'), may hold values from -8000 to 8000
- incoming_key: bfloat16 [128, 2048], P('dp', 'tensor'), may hold values from -4.5 to 4.5
- new_value: bfloat16 [128, 2048], P('dp', 'tensor'), may hold values from -4.5 to 4.5
- key_cache: bfloat16 [128, 256, 2048], P('dp', None, 'tensor'), may hold values from -4.5 to 4.5
- value_cache: bfloat16 [128, 256, 2048], P('dp', None, 'tensor'), may hold values from -4.5 to 4.5
- cache_len: int32 [128], P('dp'), may hold values from 2 to 256
- out_weight: bfloat16 [4096, 4608], P('tensor'), may hold values from -0.09375 to 0.09375
- residual: bfloat16 [128, 4608], P('dp'), may hold values from -6 to 6
- post_gain: float32 [4608], replicated, may hold values from 0.5 to 1.5
- final_gain: float32 [4608], replicated, may hold values from 0.5 to 1.5
- vocab_weight: bfloat16 [131072, 4608], P(('dp', 'tensor')), may hold values from -113 to 113
- sampled: int32 [128], P('dp'), may hold values from 0 to 131071
- stop_flag: int32 [128], P('dp'), may hold values from 0 to 1, as said below
Outputs:
- new_residual: bfloat16 [128, 4608], P('dp', 'tensor')
- token_logprob: float32 [128], P('dp')
- insert_rank: int32 [128], P('dp')
- released_slot_total: int32 [], replicated
Inputs may be any that keep to these rules, and one draw needn't show every extreme that they name: `stop_flag`: each aligned block of 16 slots holds 1 to 16 stops.
All inputs are finite; a program needn't handle non-finite values.
Results may differ from a plain program's by a relative error of at most 0.0038.
The roundings to bfloat16 on the way count: a program that leaves them out, or rounds other values in their place, can miss the bound.
Values may be sent and summed in bfloat16 or wider, within the bound.
A program may use at most 128 MiB of HBM per device.

v0:
```python
import jax
import jax.numpy as jnp
from jax import lax
from jax.sharding import PartitionSpec as P

D = 4608
HEADS = 32
KV_HEADS = 16
HEAD_DIM = 128


def prefix(part, axis, combine, identity):
    place = lax.axis_index(axis)
    gathered = lax.all_gather(part, axis)
    state = jnp.zeros_like(part) + jnp.asarray(identity, part.dtype)

    def one(lap, state):
        return combine(state, lax.dynamic_index_in_dim(gathered, lap, 0, False))

    return lax.fori_loop(0, place, one, state)


def attend_local(query, incoming_key, new_value, key_cache, value_cache, cache_len):
    slot_dev = query.shape[0]
    positions = key_cache.shape[1]
    kv_local = incoming_key.shape[1] // HEAD_DIM
    group = HEADS // KV_HEADS
    query_vector = query.reshape(slot_dev, kv_local, group, HEAD_DIM)
    keys = key_cache.reshape(slot_dev, positions, kv_local, HEAD_DIM)
    values = value_cache.reshape(slot_dev, positions, kv_local, HEAD_DIM)
    self_key = incoming_key.reshape(slot_dev, kv_local, HEAD_DIM)
    own_value = new_value.reshape(slot_dev, kv_local, HEAD_DIM).astype(jnp.float32)
    scores = (
        jnp.einsum("bkgd,bckd->bkgc", query_vector, keys, preferred_element_type=jnp.float32) / 12.0
    )
    self_entry = (
        jnp.einsum("qyxm,qym->qyx", query_vector, self_key, preferred_element_type=jnp.float32)
        / 12.0
    )
    valid = (
        jnp.arange(positions, dtype=jnp.int32)[None, None, None, :] < cache_len[:, None, None, None]
    )
    scores = jnp.where(valid, scores, -1e30)
    top = jnp.maximum(jnp.max(scores, axis=-1), self_entry)
    expo = jnp.where(valid, jnp.exp(scores - top[..., None]), 0.0)
    own_exp = jnp.exp(self_entry - top)
    total = jnp.sum(expo, axis=-1) + own_exp
    weight = (expo / total[..., None]).astype(jnp.bfloat16)
    own_weight = (own_exp / total).astype(jnp.bfloat16).astype(jnp.float32)
    attn = jnp.einsum("bkgc,bckd->bkgd", weight, values, preferred_element_type=jnp.float32)
    attn = attn + own_weight[..., None] * own_value[:, :, None, :]
    return attn.astype(jnp.bfloat16).reshape(slot_dev, kv_local * group * HEAD_DIM)


def collect_slots(hidden, sampled):
    return (
        lax.all_gather(hidden, "dp", axis=0, tiled=True),
        lax.all_gather(sampled, "dp", axis=0, tiled=True),
    )


def add_counts(earlier, later):
    return earlier + later


def on_device(
    query,
    incoming_key,
    new_value,
    key_cache,
    value_cache,
    cache_len,
    out_weight,
    residual,
    post_gain,
    final_gain,
    vocab_weight,
    sampled,
    stop_flag,
):
    slot_dev = query.shape[0]
    attn = attend_local(query, incoming_key, new_value, key_cache, value_cache, cache_len)
    partial_value = jnp.dot(attn, out_weight, preferred_element_type=jnp.float32)
    whole = lax.psum(partial_value, "tensor")
    post = whole * lax.rsqrt(jnp.mean(whole * whole, axis=1, keepdims=True) + 1e-06) * post_gain
    full_mix = (residual.astype(jnp.float32) + post).astype(jnp.bfloat16)
    mixed = full_mix.astype(jnp.float32)
    hidden = (
        mixed * lax.rsqrt(jnp.mean(mixed * mixed, axis=1, keepdims=True) + 1e-06) * final_gain
    ).astype(jnp.bfloat16)
    width = D // lax.axis_size("tensor")
    new_residual = lax.dynamic_slice_in_dim(full_mix, lax.axis_index("tensor") * width, width, 1)
    every, ids = collect_slots(hidden, sampled)
    logits = lax.dot_general(
        every, vocab_weight, (((1,), (1,)), ((), ())), preferred_element_type=jnp.float32
    )
    vocabulary_per_device = vocab_weight.shape[0]
    vocab_start = (
        lax.axis_index("dp") * lax.axis_size("tensor") + lax.axis_index("tensor")
    ) * vocabulary_per_device
    local_ids = ids - vocab_start
    hit = jnp.arange(vocabulary_per_device, dtype=jnp.int32)[None, :] == local_ids[:, None]
    picked_part = jnp.sum(jnp.where(hit, logits, 0.0), axis=1)
    row_max = jnp.max(logits, axis=1)
    freed = (stop_flag == 1).astype(jnp.int32)
    count = jnp.sum(freed)
    top = lax.pmax(row_max, ("dp", "tensor"))
    expsum, picked = lax.psum(
        (jnp.sum(jnp.exp(logits - top[:, None]), axis=1), picked_part), ("dp", "tensor")
    )
    before = prefix(count, "dp", add_counts, jnp.zeros((), jnp.int32))
    released_count = lax.psum(count.astype(jnp.float32), "dp").astype(jnp.int32)
    logprob_all = picked - (jnp.log(expsum) + top)
    token_logprob = lax.dynamic_slice_in_dim(
        logprob_all, lax.axis_index("dp") * slot_dev, slot_dev, 0
    )
    local_before = jnp.cumsum(freed) - freed + before
    insert_rank = jnp.where(freed == 1, local_before, -1).astype(jnp.int32)
    return (new_residual, token_logprob, insert_rank, released_count)


def solution(mesh):
    in_specs = (
        P("dp", "tensor"),
        P("dp", "tensor"),
        P("dp", "tensor"),
        P("dp", None, "tensor"),
        P("dp", None, "tensor"),
        P("dp"),
        P("tensor", None),
        P("dp", None),
        P(),
        P(),
        P(("dp", "tensor"), None),
        P("dp"),
        P("dp"),
    )
    out_specs = (P("dp", "tensor"), P("dp"), P("dp"), P())
    return jax.shard_map(
        on_device, mesh=mesh, in_specs=in_specs, out_specs=out_specs, check_vma=False
    )
```

profile of v0, /device:TPU:0, one launch (start us, length us, event | category | flops | bytes accessed | tf_op | source)
XLA Modules:
  0.0 203.0 jit_solution(7493364260681126007)
XLA Ops:
  7.2 0.8 reshape.101
  8.0 0.7 reshape.122
  8.7 0.7 iota_compare_fusion.1
  9.7 3.5 %fusion.28 = (f32[16,4,2]{2,1,0:T(4,128)S(1)}, f32[16,4,2,256]{3,2,1,0:T(2,128)S(1)}) fusion(bf16[16,4,2,128]{3,2,1,0:T(2,128)(2,1)S(1)} %reshape.101, pred[16,256]{1,0:T(8,128)(4,1)S(1)} %iota_compare_fusion.1, bf16[16,256,512]{2,1,0:T(8,128)(2,1)} %param.18), kind=kOutput, calls=%fused_computation.40 | convolution fusion | flops 8486784 | bytes 4362752 | tf_op jit(solution)/shard_map/bkgd,bckd->bkgc/dot_general | solution.py:34
  13.2 0.3 fusion.22
  13.5 2.9 %fusion.15 = bf16[16,4,2,128]{3,2,1,0:T(2,128)(2,1)S(1)} fusion(f32[16,4,2]{2,1,0:T(4,128)S(1)} %get-tuple-element.45, f32[16,4,128]{2,1,0:T(4,128)S(1)} %reshape.108, f32[16,4,2]{2,1,0:T(4,128)S(1)} %get-tuple-element.44, f32[16,4,2,256]{3,2,1,0:T(2,128)S(1)} %get-tuple-element.47, pred[16,256]{1,0:T(8,128)(4,1)S(1)} %iota_compare_fusion.1, ...), kind=kOutput, calls=%fused_computation.12 | convolution fusion | flops 8568832 | bytes 4396544 | tf_op jit(solution)/shard_map/bkgc,bckd->bkgd/dot_general | solution.py:50
  16.6 5.8 %fusion.31 = f32[16,4608]{1,0:T(8,128)} fusion(bf16[16,1024]{1,0:T(8,128)(2,1)S(1)} %reshape.105, bf16[1024,4608]{1,0:T(8,128)(2,1)} %param.21), kind=kOutput, calls=%fused_computation.43 | convolution fusion | flops 150994944 | bytes 9764864 | tf_op jit(solution)/shard_map/dot_general | solution.py:83
  22.5 38.7 %all-reduce.6.cloned.1.call-done = f32[16,4608]{1,0:T(8,128)} async-done(((f32[16,4608]{1,0:T(8,128)}), f32[16,4608]{1,0:T(8,128)}) %all-reduce.6.cloned.1.call-update) | async-done | bytes 294928 | tf_op jit(solution)/shard_map/psum | solution.py:84
  61.1 1.1 multiply_reduce_fusion
  62.3 1.2 fusion.18
  63.5 0.8 fusion.20
  64.3 0.6 fusion.25
  65.6 12.7 %psum.31 = f32[]{:T(128)} all-reduce(f32[]{:T(128)S(6)} %convert_element_type.54), channel_id=1, replica_groups=mesh['dp'=8,'tensor'=4] {'dp'}, use_global_device_ids=true, to_apply=%region_15.16 | all-reduce | flops 1 | bytes 8 | tf_op jit(solution)/shard_map/psum | solution.py:112
  79.2 0.6 dynamic-slice
  80.5 0.2 dynamic-update-slice
  80.7 1.4 dynamic-update-slice.1
  82.2 7.0 %all-reduce.2 = (s32[128]{0:T(128)S(1)}, s32[8]{0:T(128)S(1)}) all-reduce(s32[128]{0:T(128)S(1)} %dynamic-update-slice, s32[8]{0:T(128)S(1)} %dynamic-update-slice.1), channel_id=1, replica_groups=mesh['dp'=8,'tensor'=4] {'dp'}, use_global_device_ids=true, to_apply=%add | all-reduce | flops 136 | bytes 1088
  89.2 0.5 compare_select_fusion
  89.7 0.6 constant_dynamic-slice_fusion
  90.3 17.8 %fusion.29 = (f32[128]{0:T(128)S(1)}, f32[128,4096]{1,0:T(8,128)S(1)}) fusion(bf16[128,4608]{1,0:T(8,128)(2,1)} %all-gather.2.cloned.1.call-done, bf16[4096,4608]{1,0:T(8,128)(2,1)} %param.25), kind=kOutput, calls=%fused_computation.41 | convolution fusion | flops 4832362496 | bytes 41026048 | tf_op jit(solution)/shard_map/dot_general | solution.py:94
  108.2 46.7 %pmax.7 = f32[128]{0:T(128)S(1)} all-reduce(f32[128]{0:T(128)S(1)} %get-tuple-element.48), channel_id=1, replica_groups=mesh['dp'=8,'tensor'=4] {'dp','tensor'}, use_global_device_ids=true, to_apply=%region_8.9 | all-reduce | flops 128 | bytes 1024 | tf_op jit(solution)/shard_map/pmax | solution.py:107
  154.9 0.7 exponential_reduce_fusion
  155.6 38.8 %all-reduce.3 = (f32[128]{0:T(128)S(1)}, f32[128]{0:T(128)S(1)}) all-reduce(f32[128]{0:T(128)S(1)} %get-tuple-element.29, f32[128]{0:T(128)S(1)} %get-tuple-element.28), channel_id=1, replica_groups=mesh['dp'=8,'tensor'=4] {'dp','tensor'}, use_global_device_ids=true, to_apply=%region_6.7 | all-reduce | flops 256 | bytes 2048 | tf_op jit(solution)/shard_map/psum | solution.py:108
  194.4 0.6 dynamic_slice.11
  (35 shorter events, 0.7 us)
Async XLA Ops:
  7.2 6.3 %copy-start.3 = (bf16[16,512]{1,0:T(8,128)(2,1)S(1)}, bf16[16,512]{1,0:T(8,128)(2,1)}, u32[]{:S(2)}) copy-start(bf16[16,512]{1,0:T(8,128)(2,1)} %param.17) | copy-start | bytes 49156
  7.2 54.0 %all-reduce.6.cloned.1.call-start = ((), (), s32[]{:S(2)}) async-start(), calls=%async_computation | async-start | bytes 589824 | tf_op jit(solution)/shard_map/psum | solution.py:84
  16.5 45.8 %copy-start = (bf16[16,4608]{1,0:T(8,128)(2,1)S(1)}, bf16[16,4608]{1,0:T(8,128)(2,1)}, u32[]{:S(2)}) copy-start(bf16[16,4608]{1,0:T(8,128)(2,1)} %param.22) | copy-start | bytes 442372
  16.5 45.7 %copy-start.1 = (f32[4608]{0:T(1024)S(1)}, f32[4608]{0:T(1024)}, u32[]{:S(2)}) copy-start(f32[4608]{0:T(1024)} %param.23) | copy-start | bytes 55300
  16.5 47.0 %copy-start.2 = (f32[4608]{0:T(1024)S(1)}, f32[4608]{0:T(1024)}, u32[]{:S(2)}) copy-start(f32[4608]{0:T(1024)} %param.24) | copy-start | bytes 55300
  16.5 47.7 %copy-start.4 = (s32[16]{0:T(128)S(1)}, s32[16]{0:T(128)}, u32[]{:S(2)}) copy-start(s32[16]{0:T(128)} %param.27) | copy-start | bytes 196
  16.5 62.7 %copy-start.6 = (u32[32]{0:T(128)S(1)}, u32[32]{0:T(128)}, u32[]{:S(2)}) copy-start(u32[32]{0:T(128)} %constant.57) | copy-start | bytes 388
  16.6 63.9 %copy-start.5 = (s32[16]{0:T(128)S(1)}, s32[16]{0:T(128)}, u32[]{:S(2)}) copy-start(s32[16]{0:T(128)} %param.26) | copy-start | bytes 196
  22.4 67.9 %all-gather.2.cloned.1.call-start = ((), (), s32[]{:S(2)}) async-start(), calls=%async_computation.1 | async-start | bytes 1327104 | tf_op jit(solution)/shard_map/all_gather | solution.py:57
Sparse Core Ops, SparseCore 0:
  22.5 38.5 all-reduce.5
  64.4 23.8 all-gather.1
where the time goes:
time: 204 us; the launch traced here: 203 us
  blocking collectives  105 us (51%)
  waiting for transfers between devices  38.7 us (19%)
  matrix products  30.2 us (15%)
  between operations  17.3 us (8%)
  other arithmetic  6.21 us (3%)
  local copies, waits for them, and re-layouts  5.14 us (3%)
    pmax x1, blocking collectives, on_device(): top = lax.pmax(row_max, ('dp', 'tensor'))  46.7 us
    psum x1, blocking collectives, on_device(): lax.psum((jnp.sum(jnp.exp(logits - top[:, None]), axis=1), picked_part),...  38.8 us
    psum x1, waiting for transfers between devices, on_device(): whole = lax.psum(partial_value, 'tensor')  38.7 us
    dot_general x1, matrix products, on_device(): lax.dot_general(every, vocab_weight, (((1,), (1,)), ((), ())), preferred_...  17.8 us
    psum x1, blocking collectives, on_device(): released_count = lax.psum(count.astype(jnp.float32), 'dp').astype(jnp.int32)  12.7 us
    unnamed x1, blocking collectives  7.04 us
    dot_general x1, matrix products, on_device(): jnp.dot(attn, out_weight, preferred_element_type=jnp.float32)  5.81 us
  transfers between devices with their start and end apart: 2, of which 1 were waited for; matrix products, arithmetic and copies ran while one was open for 2% of the time, Pallas kernels for 0%

commit v1 on v0

v1 whole, which is shorter than its diff:
```python
import functools

import jax
import jax.numpy as jnp
from jax import lax
from jax.experimental import pallas as pl
from jax.experimental.pallas import tpu as pltpu
from jax.sharding import PartitionSpec as P

HEAD_DIM = 128
LANES = 128
MESH = pl.DeviceIdType.MESH
F32 = jnp.float32
BF16 = jnp.bfloat16
NT = (((1,), (1,)), ((), ()))


def chunk_count(model):
    for count in (3, 2):
        if model % (count * LANES) == 0:
            return count
    return 1


def kernel(
    dp_n,
    t_n,
    tiles,
    q_h,
    ik_h,
    nv_h,
    kc_h,
    vc_h,
    len_s,
    ow_h,
    res_h,
    pg_h,
    fg_h,
    w_h,
    samp_s,
    stop_s,
    nr_o,
    f_o,
    i_o,
    q,
    ik,
    nv,
    kc,
    vc,
    ow,
    res,
    pg,
    fg,
    w,
    attn,
    psend,
    precv,
    resf,
    zfold,
    zbuf,
    nrf,
    hbuf,
    acc,
    ibuf,
    dstat,
    zstat,
    lsem,
    wsem,
    ps,
    pr,
    zs,
    zr,
    hs,
    hr,
    isn,
    irc,
    ds,
    dr,
    es,
    er,
):
    d = lax.axis_index("dp")
    t = lax.axis_index("tensor")
    slot_dev, model = res.shape
    positions = kc.shape[1]
    heads = q.shape[1] // HEAD_DIM
    kv = ik.shape[1] // HEAD_DIM
    group = heads // kv
    rows = slot_dev // t_n
    chunks = hbuf.shape[0]
    width = model // chunks
    slots = dp_n * slot_dev
    fold = zbuf.shape[2]
    chips = dp_n // 2
    half = slot_dev // 2
    vloc = w.shape[0]
    tile = vloc // tiles

    def at_dp(peer):
        return {"dp": peer, "tensor": t}

    def at_t(peer):
        return {"dp": d, "tensor": peer}

    barrier = pltpu.get_barrier_semaphore()
    for k in range(1, dp_n):
        pl.semaphore_signal(
            barrier, inc=1, device_id=at_dp((d + k) % dp_n), device_id_type=MESH
        )
    for k in range(1, t_n):
        pl.semaphore_signal(
            barrier, inc=1, device_id=at_t((t + k) % t_n), device_id_type=MESH
        )

    def local(src, dst, i):
        copy = pltpu.make_async_copy(src, dst, lsem.at[i])
        copy.start()
        return copy

    def remote(src, dst, s, r, dev):
        return pltpu.make_async_remote_copy(
            src_ref=src, dst_ref=dst, send_sem=s, recv_sem=r, device_id=dev, device_id_type=MESH
        )

    first = pl.ds(0, half)
    second = pl.ds(half, half)
    c_q = local(q_h, q, 0)
    c_ik = local(ik_h, ik, 1)
    c_k = [local(kc_h.at[first], kc.at[first], 2)]
    c_nv = local(nv_h, nv, 3)
    c_v = [local(vc_h.at[first], vc.at[first], 4)]
    c_k.append(local(kc_h.at[second], kc.at[second], 5))
    c_v.append(local(vc_h.at[second], vc.at[second], 6))
    c_ow = local(ow_h, ow, 7)
    c_res = local(res_h, res, 8)
    c_pg = local(pg_h, pg, 9)
    c_fg = local(fg_h, fg, 10)
    w_copies = [
        pltpu.make_async_copy(
            w_h.at[pl.ds(i * tile, tile)], w.at[pl.ds(i * tile, tile)], wsem.at[i]
        )
        for i in range(tiles)
    ]
    pending = list(w_copies)

    def issue(count):
        for _ in range(min(count, len(pending))):
            pending.pop(0).start()

    lane = lax.broadcasted_iota(jnp.int32, (8, slots), 1)
    sub = lax.broadcasted_iota(jnp.int32, (8, slots), 0)
    info = jnp.zeros((8, slots), jnp.int32)
    for i in range(slot_dev):
        freed = jnp.where(stop_s[i] == 1, 1, 0)
        info = jnp.where(lane == d * slot_dev + i, jnp.where(sub == 0, samp_s[i], freed), info)
    ibuf[d] = info

    pl.semaphore_wait(barrier, dp_n - 1 + t_n - 1)
    sent = []
    i_copies = []
    for k in range(1, dp_n):
        copy = remote(
            ibuf.at[d], ibuf.at[d], isn.at[k - 1], irc.at[k - 1], at_dp((d + k) % dp_n)
        )
        copy.start()
        i_copies.append(copy)
    sent += i_copies

    head_mask = lax.broadcasted_iota(
        jnp.int32, (heads, heads * HEAD_DIM), 1
    ) // HEAD_DIM == lax.broadcasted_iota(jnp.int32, (heads, heads * HEAD_DIM), 0)
    pos = lax.broadcasted_iota(jnp.int32, (heads, positions), 1)
    c_q.wait()
    c_ik.wait()
    qf = q[...].astype(F32)
    ikf = ik[...].astype(F32)
    for part in range(2):
        numbers = range(part * half, part * half + half)
        c_k[part].wait()
        issue(1)
        scores = []
        for b in numbers:
            x = jnp.where(head_mask, jnp.broadcast_to(qf[b : b + 1, :], head_mask.shape), 0.0)
            blocks = []
            for g in range(kv):
                block = x[:, g * group * HEAD_DIM : (g * group + 1) * HEAD_DIM]
                for j in range(g * group + 1, (g + 1) * group):
                    block = block + x[:, j * HEAD_DIM : (j + 1) * HEAD_DIM]
                blocks.append(block)
            spread = jnp.concatenate(blocks, axis=1)
            score = lax.dot_general(
                spread.astype(BF16), kc[b], NT, preferred_element_type=F32
            ) / 12.0
            own = jnp.sum(spread * ikf[b : b + 1, :], axis=1, keepdims=True) / 12.0
            scores.append((score, own))
        weights = []
        for b, (score, own) in zip(numbers, scores):
            valid = pos < len_s[b]
            score = jnp.where(valid, score, -1e30)
            top = jnp.maximum(jnp.max(score, axis=1, keepdims=True), own)
            expo = jnp.where(valid, jnp.exp(score - top), 0.0)
            own_exp = jnp.exp(own - top)
            total = jnp.sum(expo, axis=1, keepdims=True) + own_exp
            weights.append(((expo / total).astype(BF16), (own_exp / total).astype(BF16).astype(F32)))
        if part == 0:
            c_nv.wait()
            nvf = nv[...].astype(F32)
        c_v[part].wait()
        issue(1)
        for b, (weight, own) in zip(numbers, weights):
            mix = jnp.dot(weight, vc[b], preferred_element_type=F32) + own * nvf[b : b + 1, :]
            for h in range(heads):
                g = h // group
                attn[b : b + 1, h * HEAD_DIM : (h + 1) * HEAD_DIM] = mix[
                    h : h + 1, g * HEAD_DIM : (g + 1) * HEAD_DIM
                ]

    issue(1)
    c_res.wait()
    res_all = res[...].astype(F32)
    for s in range(t_n):
        resf[s] = res_all[s * rows : (s + 1) * rows, :]
    attn_b = attn[...].astype(BF16)
    c_ow.wait()
    issue(len(pending))
    for c in range(chunks):
        cols = slice(c * width, (c + 1) * width)
        partial = jnp.dot(attn_b, ow[:, cols], preferred_element_type=F32)
        for s in range(t_n):
            psend[s, :, cols] = partial[s * rows : (s + 1) * rows, :]
    p_copies = []
    for k in range(1, t_n):
        peer = (t + k) % t_n
        copy = remote(psend.at[peer], precv.at[k - 1], ps.at[k - 1], pr.at[k - 1], at_t(peer))
        copy.start()
        p_copies.append(copy)
    sent += p_copies
    c_pg.wait()
    c_fg.wait()
    proj = psend[t]
    for k in range(1, t_n):
        p_copies[k - 1].wait_recv()
        proj = proj + precv[k - 1]
    post = proj * lax.rsqrt(jnp.mean(proj * proj, axis=1, keepdims=True) + 1e-06) * pg[...]
    mixed = (resf[t] + post).astype(BF16).astype(F32)
    if t_n * fold != model:
        zfold[...] = jnp.zeros_like(zfold)
    for s in range(t_n):
        size = min(fold, model - s * fold)
        if size > 0:
            zfold[s * rows : (s + 1) * rows, 0:size] = mixed[:, s * fold : s * fold + size]
    zbuf[t] = zfold[...].astype(BF16)
    z_copies = []
    for k in range(1, t_n):
        copy = remote(
            zbuf.at[t], zbuf.at[t], zs.at[k - 1], zr.at[k - 1], at_t((t + k) % t_n)
        )
        copy.start()
        z_copies.append(copy)
    sent += z_copies
    for copy in z_copies:
        copy.wait_recv()
    for s in range(t_n):
        piece = zbuf[s].astype(F32)
        for f in range(t_n):
            size = min(fold, model - f * fold)
            if size > 0:
                nrf[s * rows : (s + 1) * rows, f * fold : f * fold + size] = piece[
                    f * rows : (f + 1) * rows, 0:size
                ]
    mixed = nrf[...]
    nr_o[...] = mixed.astype(BF16)
    hidden = (
        mixed * lax.rsqrt(jnp.mean(mixed * mixed, axis=1, keepdims=True) + 1e-06) * fg[...]
    ).astype(BF16)

    sibling = d + 1 - 2 * (d % 2)
    direct = {}
    for c in range(chunks):
        hbuf[c, d] = hidden[:, c * width : (c + 1) * width]
        here = hbuf.at[c, d]
        for k in range(1, chips):
            direct[c, k] = remote(
                here, here, hs.at[c, k], hr.at[c, k], at_dp((d + 2 * k) % dp_n)
            )
            direct[c, k].start()
        direct[c, 0] = remote(here, here, hs.at[c, 0], hr.at[c, 0], at_dp(sibling))
        direct[c, 0].start()
    sent += list(direct.values())
    passed = {}

    def pass_on(c):
        for k in range(1, chips):
            direct[c, k].wait_recv()
            there = hbuf.at[c, (d + dp_n - 2 * k) % dp_n]
            j = chips - 1 + k
            passed[c, k] = remote(there, there, hs.at[c, j], hr.at[c, j], at_dp(sibling))
            passed[c, k].start()
            sent.append(passed[c, k])

    for copy in i_copies:
        copy.wait_recv()
    info = ibuf[0]
    for j in range(1, dp_n):
        info = info + ibuf[j]
    flags = info[1:2, :]
    order = lax.broadcasted_iota(jnp.int32, (slots, slots), 0) < lax.broadcasted_iota(
        jnp.int32, (slots, slots), 1
    )
    flags8 = jnp.broadcast_to(flags, (8, slots)).astype(F32)
    before = jnp.dot(
        flags8.astype(BF16),
        jnp.where(order, 1.0, 0.0).astype(BF16),
        preferred_element_type=F32,
    )
    rank = jnp.where(flags8 > 0.5, before, -1.0)
    count = jnp.sum(flags8, axis=1, keepdims=True)
    i_o[...] = jnp.where(sub == 0, rank, count).astype(jnp.int32)
    start = (d * t_n + t) * vloc
    local_ids = info[0:1, :] - start

    pass_on(0)
    top = None
    for c in range(chunks):
        direct[c, 0].wait_recv()
        for k in range(1, chips):
            passed[c, k].wait_recv()
        state = hbuf[c].reshape(slots, width)
        for i in range(tiles):
            if c == 0:
                w_copies[i].wait()
            if c + 1 < chunks and i == tiles // 2:
                pass_on(c + 1)
            part = lax.dot_general(
                w[i * tile : (i + 1) * tile, c * width : (c + 1) * width],
                state,
                NT,
                preferred_element_type=F32,
            )
            if c > 0:
                part = part + acc[i * tile : (i + 1) * tile, :]
            if c + 1 < chunks:
                acc[i * tile : (i + 1) * tile, :] = part
                continue
            index = lax.broadcasted_iota(jnp.int32, (tile, slots), 0) + i * tile
            hit = jnp.sum(jnp.where(index == local_ids, part, 0.0), axis=0, keepdims=True)
            peak = jnp.max(part, axis=0, keepdims=True)
            if top is None:
                top = peak
                total = jnp.sum(jnp.exp(part - top), axis=0, keepdims=True)
                picked = hit
            else:
                larger = jnp.maximum(top, peak)
                total = total * jnp.exp(top - larger) + jnp.sum(
                    jnp.exp(part - larger), axis=0, keepdims=True
                )
                top = larger
                picked = picked + hit

    def pack(top, total, picked):
        return jnp.where(sub == 0, top, jnp.where(sub == 1, total, picked))

    def merge(parts):
        top = parts[0][0:1, :]
        for part in parts[1:]:
            top = jnp.maximum(top, part[0:1, :])
        total = jnp.zeros_like(top)
        picked = jnp.zeros_like(top)
        for part in parts:
            total = total + part[1:2, :] * jnp.exp(part[0:1, :] - top)
            picked = picked + part[2:3, :]
        return top, total, picked

    dstat[d] = pack(top, total, picked)
    copies = []
    for k in range(1, dp_n):
        copy = remote(dstat.at[d], dstat.at[d], ds.at[k - 1], dr.at[k - 1], at_dp((d + k) % dp_n))
        copy.start()
        copies.append(copy)
    for copy in copies:
        copy.wait_recv()
    sent += copies
    zstat[t] = pack(*merge([dstat[j] for j in range(dp_n)]))
    copies = []
    for k in range(1, t_n):
        copy = remote(zstat.at[t], zstat.at[t], es.at[k - 1], er.at[k - 1], at_t((t + k) % t_n))
        copy.start()
        copies.append(copy)
    for copy in copies:
        copy.wait_recv()
    sent += copies
    top, total, picked = merge([zstat[j] for j in range(t_n)])
    f_o[...] = jnp.broadcast_to(picked - (jnp.log(total) + top), (8, slots))
    for copy in sent:
        copy.wait_send()


def on_device(
    dp_n,
    t_n,
    query,
    incoming_key,
    new_value,
    key_cache,
    value_cache,
    cache_len,
    out_weight,
    residual,
    post_gain,
    final_gain,
    vocab_weight,
    sampled,
    stop_flag,
):
    slot_dev, model = residual.shape
    slots = slot_dev * dp_n
    rows = slot_dev // t_n
    fold = -(-model // (t_n * LANES)) * LANES
    chunks = chunk_count(model)
    vloc = vocab_weight.shape[0]
    tiles = max(1, vloc // 512)
    dma = pltpu.SemaphoreType.DMA
    anywhere = pl.BlockSpec(memory_space=pl.ANY)
    smem = pl.BlockSpec(memory_space=pltpu.SMEM)
    vmem = pl.BlockSpec(memory_space=pltpu.VMEM)

    def like(a):
        return pltpu.VMEM(a.shape, a.dtype)

    pg = post_gain.reshape(1, model)
    fg = final_gain.reshape(1, model)
    mixed, logs, ranks = pl.pallas_call(
        functools.partial(kernel, dp_n, t_n, tiles),
        out_shape=(
            jax.ShapeDtypeStruct((slot_dev, model), BF16),
            jax.ShapeDtypeStruct((8, slots), F32),
            jax.ShapeDtypeStruct((8, slots), jnp.int32),
        ),
        in_specs=[anywhere] * 5 + [smem] + [anywhere] * 5 + [smem] * 2,
        out_specs=(vmem,) * 3,
        scratch_shapes=[
            like(query),
            like(incoming_key),
            like(new_value),
            like(key_cache),
            like(value_cache),
            like(out_weight),
            like(residual),
            like(pg),
            like(fg),
            like(vocab_weight),
            pltpu.VMEM(query.shape, F32),
            pltpu.VMEM((t_n, rows, model), F32),
            pltpu.VMEM((t_n - 1, rows, model), F32),
            pltpu.VMEM((t_n, rows, model), F32),
            pltpu.VMEM((slot_dev, fold), F32),
            pltpu.VMEM((t_n, slot_dev, fold), BF16),
            pltpu.VMEM((slot_dev, model), F32),
            pltpu.VMEM((chunks, dp_n, slot_dev, model // chunks), BF16),
            pltpu.VMEM((vloc, slots), F32),
            pltpu.VMEM((dp_n, 8, slots), jnp.int32),
            pltpu.VMEM((dp_n, 8, slots), F32),
            pltpu.VMEM((t_n, 8, slots), F32),
            dma((11,)),
            dma((tiles,)),
            dma((t_n - 1,)),
            dma((t_n - 1,)),
            dma((t_n - 1,)),
            dma((t_n - 1,)),
            dma((chunks, dp_n - 1)),
            dma((chunks, dp_n - 1)),
            dma((dp_n - 1,)),
            dma((dp_n - 1,)),
            dma((dp_n - 1,)),
            dma((dp_n - 1,)),
            dma((t_n - 1,)),
            dma((t_n - 1,)),
        ],
        compiler_params=pltpu.CompilerParams(
            collective_id=0, has_side_effects=True, vmem_limit_bytes=62 * 1024 * 1024
        ),
    )(
        query,
        incoming_key,
        new_value,
        key_cache,
        value_cache,
        cache_len,
        out_weight,
        residual,
        pg,
        fg,
        vocab_weight,
        sampled,
        stop_flag,
    )
    share = model // t_n
    new_residual = lax.dynamic_slice_in_dim(mixed, lax.axis_index("tensor") * share, share, 1)
    begin = lax.axis_index("dp") * slot_dev
    token_logprob = lax.dynamic_slice(logs, (0, begin), (1, slot_dev))[0]
    insert_rank = lax.dynamic_slice(ranks, (0, begin), (1, slot_dev))[0]
    return (new_residual, token_logprob, insert_rank, ranks[1, 0])


def solution(mesh):
    in_specs = (
        P("dp", "tensor"),
        P("dp", "tensor"),
        P("dp", "tensor"),
        P("dp", None, "tensor"),
        P("dp", None, "tensor"),
        P("dp"),
        P("tensor", None),
        P("dp", None),
        P(),
        P(),
        P(("dp", "tensor"), None),
        P("dp"),
        P("dp"),
    )
    out_specs = (P("dp", "tensor"), P("dp"), P("dp"), P())
    return jax.shard_map(
        functools.partial(on_device, mesh.shape["dp"], mesh.shape["tensor"]),
        mesh=mesh,
        in_specs=in_specs,
        out_specs=out_specs,
        check_vma=False,
    )
```

time: 204 us -> 60.9 us (0.30)
  blocking collectives: 105 us -> 0 us
  Pallas kernels: 0 us -> 52.1 us
  waiting for transfers between devices: 38.7 us -> 0 us
  matrix products: 30.2 us -> 0 us
  between operations: 17.3 us -> 0.65 us
  other arithmetic: 6.21 us -> 0 us
  local copies, waits for them, and re-layouts: 5.14 us -> 7.77 us
    pallas_call x0 -> x1, Pallas kernels: none -> 52.1 us  [on_device(): pl.pallas_call(functools.partial(kernel, dp_n, t_n, tiles), out_shape=(ja...]
    psum x2 -> x0, blocking collectives: 51.6 us -> none  [the longest x1 38.8 us: on_device(): lax.psum((jnp.sum(jnp.exp(logits - top[:, None]), axis=1), picked_part),...]
    pmax x1 -> x0, blocking collectives: 46.7 us -> none  [on_device(): top = lax.pmax(row_max, ('dp', 'tensor'))]
    psum x1 -> x0, waiting for transfers between devices: 38.7 us -> none  [on_device(): whole = lax.psum(partial_value, 'tensor')]
    dot_general x5 -> x0, matrix products: 30.2 us -> none  [the longest x1 17.8 us: on_device(): lax.dot_general(every, vocab_weight, (((1,), (1,)), ((), ())), preferred_...]
    unnamed x1 -> x0, blocking collectives: 7.04 us -> none
    reduce_sum x5 -> x0, other arithmetic: 3.94 us -> none  [the longest x1 1.2 us: on_device(): jnp.mean(mixed * mixed, axis=1, keepdims=True) + 1e-06]
    squeeze x0 -> x2, local copies, waits for them, and re-layouts: none -> 2.51 us  [the longest x1 1.26 us: on_device(): insert_rank = lax.dynamic_slice(ranks, (0, begin), (1, slot_dev))[0]]
  transfers between devices with their start and end apart: 2 -> 0, of which waited for: 1 -> 0; matrix products, arithmetic and copies ran while one was open for 2% -> 0% of each run, Pallas kernels for 0% -> 0%
where the time goes in v1:
time: 60.9 us; the launch traced here: 60.5 us
  Pallas kernels  52.1 us (86%)
  local copies, waits for them, and re-layouts  7.77 us (13%)
  between operations  0.65 us (1%)
    pallas_call x1, Pallas kernels, on_device(): pl.pallas_call(functools.partial(kernel, dp_n, t_n, tiles), out_shape=(ja...  52.1 us
    dynamic_slice x1, local copies, waits for them, and re-layouts, on_device(): lax.dynamic_slice_in_dim(mixed, lax.axis_index('tensor') * share, share, 1)  1.39 us
    reshape x1, local copies, waits for them, and re-layouts, on_device(): pg = post_gain.reshape(1, model)  1.35 us
    reshape x1, local copies, waits for them, and re-layouts, on_device(): fg = final_gain.reshape(1, model)  1.34 us
    squeeze x1, local copies, waits for them, and re-layouts, on_device(): insert_rank = lax.dynamic_slice(ranks, (0, begin), (1, slot_dev))[0]  1.26 us
    squeeze x1, local copies, waits for them, and re-layouts, on_device(): token_logprob = lax.dynamic_slice(logs, (0, begin), (1, slot_dev))[0]  1.25 us

profile of v1, /device:TPU:0, one launch (start us, length us, event | category | flops | bytes accessed | tf_op | source)
XLA Modules:
  0.0 60.5 jit_solution(4498560685287071800)
XLA Ops:
  0.6 1.3 %reshape.14.pg_h = f32[1,4608]{1,0:T(1,128)} reshape(f32[4608]{0:T(1024)} %param.21) | data formatting | bytes 36864 | tf_op jit(solution)/shard_map/reshape | solution.py:430
  2.0 1.3 %reshape.15.fg_h = f32[1,4608]{1,0:T(1,128)} reshape(f32[4608]{0:T(1024)} %param.22) | data formatting | bytes 36864 | tf_op jit(solution)/shard_map/reshape | solution.py:431
  3.3 52.1 %shard_map.156 = (bf16[16,4608]{1,0:T(8,128)(2,1)}, f32[8,128]{1,0:T(8,128)}, s32[8,128]{1,0:T(8,128)}) custom-call(bf16[16,1024]{1,0:T(8,128)(2,1)} %q_h.1, bf16[16,512]{1,0:T(8,128)(2,1)} %ik_h.1, bf16[16,512]{1,0:T(8,128)(2,1)} %nv_h.1, bf16[16,256,512]{2,1,0:T(8,128)(2,1)} %kc_h.1, bf16[16,256,512]{2,1,0:T(8,128)(2,1)} %vc_h.1, s32[16]{0:T(128)} %len_s.1, ...), custom_call_target="tpu_custom_call" | custom-call | tf_op jit(solution)/shard_map/pallas_call | solution.py:432
  55.5 1.3 %fusion.1 = s32[16]{0:T(128)} fusion(s32[8,128]{1,0:T(8,128)} %get-tuple-element.9, s32[]{:T(128)S(6)} %select_n.8), kind=kLoop, calls=%fused_computation.4 | loop fusion | bytes 132 | tf_op jit(solution)/shard_map/squeeze | solution.py:501
  56.7 1.3 %fusion = f32[16]{0:T(128)} fusion(f32[8,128]{1,0:T(8,128)} %get-tuple-element.8, s32[]{:T(128)S(6)} %select_n.8), kind=kLoop, calls=%fused_computation.3 | loop fusion | bytes 132 | tf_op jit(solution)/shard_map/squeeze | solution.py:500
  58.0 1.4 %constant_dynamic-slice_fusion.2 = bf16[16,1152]{1,0:T(8,128)(2,1)} fusion(bf16[16,4608]{1,0:T(8,128)(2,1)} %get-tuple-element.7, s32[]{:T(128)S(6)} %select_n.7), kind=kLoop, calls=%fused_computation.2 | loop fusion | bytes 73732 | tf_op jit(solution)/shard_map/dynamic_slice | solution.py:498
  59.4 1.2 %slice.3 = s32[1,1]{1,0:T(1,128)} slice(s32[8,128]{1,0:T(8,128)} %get-tuple-element.9), slice={[1:2], [0:1]} | slice | bytes 8 | tf_op jit(solution)/shard_map/slice | solution.py:502

commit v2 on v1

--- a/solution.py
+++ b/solution.py
@@ -53,8 +53,10 @@
     fg,
     w,
     attn,
+    pfold,
     psend,
     precv,
+    psum,
     resf,
     zfold,
     zbuf,
@@ -223,11 +225,21 @@
     attn_b = attn[...].astype(BF16)
     c_ow.wait()
     issue(len(pending))
-    for c in range(chunks):
-        cols = slice(c * width, (c + 1) * width)
-        partial = jnp.dot(attn_b, ow[:, cols], preferred_element_type=F32)
-        for s in range(t_n):
-            psend[s, :, cols] = partial[s * rows : (s + 1) * rows, :]
+    padded = t_n * fold != model
+    if padded:
+        pfold[...] = jnp.zeros_like(pfold)
+        zfold[...] = jnp.zeros_like(zfold)
+    sizes = [min(fold, model - f * fold) for f in range(t_n)]
+    for f in range(t_n):
+        if sizes[f] > 0:
+            partial = jnp.dot(
+                attn_b, ow[:, f * fold : f * fold + sizes[f]], preferred_element_type=F32
+            )
+            for s in range(t_n):
+                pfold[s, f * rows : (f + 1) * rows, 0 : sizes[f]] = partial[
+                    s * rows : (s + 1) * rows, :
+                ]
+    psend[...] = pfold[...].astype(BF16)
     p_copies = []
     for k in range(1, t_n):
         peer = (t + k) % t_n
@@ -237,14 +249,19 @@
     sent += p_copies
     c_pg.wait()
     c_fg.wait()
-    proj = psend[t]
+    folded = pfold[t]
     for k in range(1, t_n):
         p_copies[k - 1].wait_recv()
-        proj = proj + precv[k - 1]
-    post = proj * lax.rsqrt(jnp.mean(proj * proj, axis=1, keepdims=True) + 1e-06) * pg[...]
+        folded = folded + precv[k - 1].astype(F32)
+    for f in range(t_n):
+        if sizes[f] > 0:
+            psum[:, f * fold : f * fold + sizes[f]] = folded[
+                f * rows : (f + 1) * rows, 0 : sizes[f]
+            ]
+    proj = psum[...]
+    post_gain = pg[...].reshape(1, model)
+    post = proj * lax.rsqrt(jnp.mean(proj * proj, axis=1, keepdims=True) + 1e-06) * post_gain
     mixed = (resf[t] + post).astype(BF16).astype(F32)
-    if t_n * fold != model:
-        zfold[...] = jnp.zeros_like(zfold)
     for s in range(t_n):
         size = min(fold, model - s * fold)
         if size > 0:
@@ -269,9 +286,9 @@
                     f * rows : (f + 1) * rows, 0:size
                 ]
     mixed = nrf[...]
-    nr_o[...] = mixed.astype(BF16)
+    final_gain = fg[...].reshape(1, model)
     hidden = (
-        mixed * lax.rsqrt(jnp.mean(mixed * mixed, axis=1, keepdims=True) + 1e-06) * fg[...]
+        mixed * lax.rsqrt(jnp.mean(mixed * mixed, axis=1, keepdims=True) + 1e-06) * final_gain
     ).astype(BF16)
 
     sibling = d + 1 - 2 * (d % 2)
@@ -297,6 +314,18 @@
             passed[c, k] = remote(there, there, hs.at[c, j], hr.at[c, j], at_dp(sibling))
             passed[c, k].start()
             sent.append(passed[c, k])
+
+    share = model // t_n
+    mine = nrf[:, 0:share]
+    for s in range(1, t_n):
+        mine = jnp.where(t == s, nrf[:, s * share : (s + 1) * share], mine)
+    nr_o[...] = mine.astype(BF16)
+
+    def own_slots(row):
+        kept = row[:, 0:slot_dev]
+        for j in range(1, dp_n):
+            kept = jnp.where(d == j, row[:, j * slot_dev : (j + 1) * slot_dev], kept)
+        return kept
 
     for copy in i_copies:
         copy.wait_recv()
@@ -315,7 +344,7 @@
     )
     rank = jnp.where(flags8 > 0.5, before, -1.0)
     count = jnp.sum(flags8, axis=1, keepdims=True)
-    i_o[...] = jnp.where(sub == 0, rank, count).astype(jnp.int32)
+    i_o[...] = own_slots(jnp.where(sub == 0, rank, count)).astype(jnp.int32)
     start = (d * t_n + t) * vloc
     local_ids = info[0:1, :] - start
 
@@ -390,9 +419,16 @@
         copy.wait_recv()
     sent += copies
     top, total, picked = merge([zstat[j] for j in range(t_n)])
-    f_o[...] = jnp.broadcast_to(picked - (jnp.log(total) + top), (8, slots))
+    f_o[...] = own_slots(jnp.broadcast_to(picked - (jnp.log(total) + top), (8, slots)))
     for copy in sent:
         copy.wait_send()
+
+
+def finish(mixed, logs, ranks, new_residual, token_logprob, insert_rank, total):
+    new_residual[...] = mixed[...]
+    token_logprob[...] = logs[0, :]
+    insert_rank[...] = ranks[0, :]
+    total[...] = ranks[1:2, 0:1]
 
 
 def on_device(
@@ -427,14 +463,13 @@
     def like(a):
         return pltpu.VMEM(a.shape, a.dtype)
 
-    pg = post_gain.reshape(1, model)
-    fg = final_gain.reshape(1, model)
+    share = model // t_n
     mixed, logs, ranks = pl.pallas_call(
         functools.partial(kernel, dp_n, t_n, tiles),
         out_shape=(
-            jax.ShapeDtypeStruct((slot_dev, model), BF16),
-            jax.ShapeDtypeStruct((8, slots), F32),
-            jax.ShapeDtypeStruct((8, slots), jnp.int32),
+            jax.ShapeDtypeStruct((slot_dev, share), BF16),
+            jax.ShapeDtypeStruct((8, slot_dev), F32),
+            jax.ShapeDtypeStruct((8, slot_dev), jnp.int32),
         ),
         in_specs=[anywhere] * 5 + [smem] + [anywhere] * 5 + [smem] * 2,
         out_specs=(vmem,) * 3,
@@ -446,12 +481,14 @@
             like(value_cache),
             like(out_weight),
             like(residual),
-            like(pg),
-            like(fg),
+            like(post_gain),
+            like(final_gain),
             like(vocab_weight),
             pltpu.VMEM(query.shape, F32),
-            pltpu.VMEM((t_n, rows, model), F32),
-            pltpu.VMEM((t_n - 1, rows, model), F32),
+            pltpu.VMEM((t_n, slot_dev, fold), F32),
+            pltpu.VMEM((t_n, slot_dev, fold), BF16),
+            pltpu.VMEM((t_n - 1, slot_dev, fold), BF16),
+            pltpu.VMEM((rows, model), F32),
             pltpu.VMEM((t_n, rows, model), F32),
             pltpu.VMEM((slot_dev, fold), F32),
             pltpu.VMEM((t_n, slot_dev, fold), BF16),
@@ -488,18 +525,24 @@
         cache_len,
         out_weight,
         residual,
-        pg,
-        fg,
+        post_gain,
+        final_gain,
         vocab_weight,
         sampled,
         stop_flag,
     )
-    share = model // t_n
-    new_residual = lax.dynamic_slice_in_dim(mixed, lax.axis_index("tensor") * share, share, 1)
-    begin = lax.axis_index("dp") * slot_dev
-    token_logprob = lax.dynamic_slice(logs, (0, begin), (1, slot_dev))[0]
-    insert_rank = lax.dynamic_slice(ranks, (0, begin), (1, slot_dev))[0]
-    return (new_residual, token_logprob, insert_rank, ranks[1, 0])
+    new_residual, token_logprob, insert_rank, total = pl.pallas_call(
+        finish,
+        out_shape=(
+            jax.ShapeDtypeStruct((slot_dev, share), BF16),
+            jax.ShapeDtypeStruct((slot_dev,), F32),
+            jax.ShapeDtypeStruct((slot_dev,), jnp.int32),
+            jax.ShapeDtypeStruct((1, 1), jnp.int32),
+        ),
+        in_specs=[vmem] * 3,
+        out_specs=(vmem,) * 4,
+    )(mixed, logs, ranks)
+    return (new_residual, token_logprob, insert_rank, total.reshape(()))
 
 
 def solution(mesh):

time: 60.9 us -> 51.4 us (0.84)
  local copies, waits for them, and re-layouts: 7.77 us -> 0 us
  Pallas kernels: 52.1 us -> 50.5 us
    pallas_call x1, Pallas kernels: 52.1 us -> 49.1 us  [on_device(): pl.pallas_call(functools.partial(kernel, dp_n, t_n, tiles), out_shape=(ja...]
    reshape x2 -> x0, local copies, waits for them, and re-layouts: 2.68 us -> none  [the longest x1 1.35 us: on_device(): pg = post_gain.reshape(1, model)]
    squeeze x2 -> x0, local copies, waits for them, and re-layouts: 2.51 us -> none  [the longest x1 1.26 us: on_device(): insert_rank = lax.dynamic_slice(ranks, (0, begin), (1, slot_dev))[0]]
    pallas_call x0 -> x1, Pallas kernels: none -> 1.4 us  [on_device(): pl.pallas_call(finish, out_shape=(jax.ShapeDtypeStruct((slot_dev, share),...]
    dynamic_slice x1 -> x0, local copies, waits for them, and re-layouts: 1.39 us -> none  [on_device(): lax.dynamic_slice_in_dim(mixed, lax.axis_index('tensor') * share, share, 1)]
    slice x1 -> x0, local copies, waits for them, and re-layouts: 1.18 us -> none  [on_device(): return (new_residual, token_logprob, insert_rank, ranks[1, 0])]
where the time goes in v2:
time: 51.4 us; the launch traced here: 51.2 us
  Pallas kernels  50.5 us (98%)
  between operations  0.64 us (1%)
    pallas_call x1, Pallas kernels, on_device(): pl.pallas_call(functools.partial(kernel, dp_n, t_n, tiles), out_shape=(ja...  49.1 us
    pallas_call x1, Pallas kernels, on_device(): pl.pallas_call(finish, out_shape=(jax.ShapeDtypeStruct((slot_dev, share),...  1.4 us

profile of v2, /device:TPU:0, one launch (start us, length us, event | category | flops | bytes accessed | tf_op | source)
XLA Modules:
  0.0 51.2 jit_solution(8853209548588303507)
XLA Ops:
  0.6 49.1 %shard_map.156 = (bf16[16,1152]{1,0:T(8,128)(2,1)}, f32[8,16]{1,0:T(8,128)}, s32[8,16]{1,0:T(8,128)}) custom-call(bf16[16,1024]{1,0:T(8,128)(2,1)} %q_h.1, bf16[16,512]{1,0:T(8,128)(2,1)} %ik_h.1, bf16[16,512]{1,0:T(8,128)(2,1)} %nv_h.1, bf16[16,256,512]{2,1,0:T(8,128)(2,1)} %kc_h.1, bf16[16,256,512]{2,1,0:T(8,128)(2,1)} %vc_h.1, s32[16]{0:T(128)} %len_s.1, ...), custom_call_target="tpu_custom_call" | custom-call | tf_op jit(solution)/shard_map/pallas_call | solution.py:467
  49.8 1.4 %shard_map.157 = (bf16[16,1152]{1,0:T(8,128)(2,1)}, f32[16]{0:T(128)}, s32[16]{0:T(128)}, s32[1,1]{1,0:T(1,128)}) custom-call(bf16[16,1152]{1,0:T(8,128)(2,1)} %get-tuple-element.11.mixed, f32[8,16]{1,0:T(8,128)} %get-tuple-element.12.logs, s32[8,16]{1,0:T(8,128)} %get-tuple-element.13.ranks), custom_call_target="tpu_custom_call" | custom-call | tf_op jit(solution)/shard_map/pallas_call | solution.py:534

commit v3 on v2

--- a/solution.py
+++ b/solution.py
@@ -348,6 +348,9 @@
     start = (d * t_n + t) * vloc
     local_ids = info[0:1, :] - start
 
+    join = 2 if tiles % 2 == 0 else 1
+    block = tile * join
+    blocks = tiles // join
     pass_on(0)
     top = None
     for c in range(chunks):
@@ -355,23 +358,24 @@
         for k in range(1, chips):
             passed[c, k].wait_recv()
         state = hbuf[c].reshape(slots, width)
-        for i in range(tiles):
+        for i in range(blocks):
             if c == 0:
-                w_copies[i].wait()
-            if c + 1 < chunks and i == tiles // 2:
+                for copy in w_copies[i * join : (i + 1) * join]:
+                    copy.wait()
+            if c + 1 < chunks and i == blocks // 2:
                 pass_on(c + 1)
             part = lax.dot_general(
-                w[i * tile : (i + 1) * tile, c * width : (c + 1) * width],
+                w[i * block : (i + 1) * block, c * width : (c + 1) * width],
                 state,
                 NT,
                 preferred_element_type=F32,
             )
             if c > 0:
-                part = part + acc[i * tile : (i + 1) * tile, :]
+                part = part + acc[i * block : (i + 1) * block, :]
             if c + 1 < chunks:
-                acc[i * tile : (i + 1) * tile, :] = part
+                acc[i * block : (i + 1) * block, :] = part
                 continue
-            index = lax.broadcasted_iota(jnp.int32, (tile, slots), 0) + i * tile
+            index = lax.broadcasted_iota(jnp.int32, (block, slots), 0) + i * block
             hit = jnp.sum(jnp.where(index == local_ids, part, 0.0), axis=0, keepdims=True)
             peak = jnp.max(part, axis=0, keepdims=True)
             if top is None:

time: 51.4 us -> 51.4 us (level)
  no operation moved by 1% of the time
where the time goes in v3:
time: 51.4 us; the launch traced here: 51.2 us
  Pallas kernels  50.6 us (98%)
  between operations  0.64 us (1%)
    pallas_call x1, Pallas kernels, on_device(): pl.pallas_call(functools.partial(kernel, dp_n, t_n, tiles), out_shape=(ja...  49.2 us
    pallas_call x1, Pallas kernels, on_device(): pl.pallas_call(finish, out_shape=(jax.ShapeDtypeStruct((slot_dev, share),...  1.4 us

profile of v3, /device:TPU:0, one launch (start us, length us, event | category | flops | bytes accessed | tf_op | source)
XLA Modules:
  0.0 51.2 jit_solution(3740679067817851822)
XLA Ops:
  0.6 49.2 %shard_map.156 = (bf16[16,1152]{1,0:T(8,128)(2,1)}, f32[8,16]{1,0:T(8,128)}, s32[8,16]{1,0:T(8,128)}) custom-call(bf16[16,1024]{1,0:T(8,128)(2,1)} %q_h.1, bf16[16,512]{1,0:T(8,128)(2,1)} %ik_h.1, bf16[16,512]{1,0:T(8,128)(2,1)} %nv_h.1, bf16[16,256,512]{2,1,0:T(8,128)(2,1)} %kc_h.1, bf16[16,256,512]{2,1,0:T(8,128)(2,1)} %vc_h.1, s32[16]{0:T(128)} %len_s.1, ...), custom_call_target="tpu_custom_call" | custom-call | tf_op jit(solution)/shard_map/pallas_call | solution.py:471
  49.8 1.4 %shard_map.157 = (bf16[16,1152]{1,0:T(8,128)(2,1)}, f32[16]{0:T(128)}, s32[16]{0:T(128)}, s32[1,1]{1,0:T(1,128)}) custom-call(bf16[16,1152]{1,0:T(8,128)(2,1)} %get-tuple-element.11.mixed, f32[8,16]{1,0:T(8,128)} %get-tuple-element.12.logs, s32[8,16]{1,0:T(8,128)} %get-tuple-element.13.ranks), custom_call_target="tpu_custom_call" | custom-call | tf_op jit(solution)/shard_map/pallas_call | solution.py:538
